TPU v7x, 32 devices: a whole 2x2x4 slice. The times are simulated.
32 devices in a mesh: groups: 2 (over x), dp: 8 (over z, y), layer: 2 (over core).
Axes of the slice: x: 2, y: 2, z: 4, core: 2. Of those that a mesh axis runs over, the one named last changes fastest.
Arguments:
- store: float32 [2, 8192, 4096], P('layer', ('groups', 'dp')), parts along dimension 1, may hold values from -0.09375 to 0.09375
- queries: float32 [2, 256, 4096], P('layer', 'dp'), may hold values from -6 to 6
- second_moment: float32 [2, 4096], P('layer'), may hold values from 0.25 to 4
- layer_rate: float32 [2], P('layer'), may hold values from 0.5 to 2
- query_task: int32 [256, 1], replicated, may hold values from 0 to 15
Outputs:
- best: float32 [16, 8192], P(None, ('groups', 'dp')), parts along dimension 1
There are 2 independent parts, one for each index of `groups`. A program takes and returns all parts, laid end to end along the dimension named above; an argument that names none is the same for every part. Nothing has to cross between parts.
Inputs may be any that keep to these rules, and one draw needn't show every extreme that they name: `query_task`: every task 0 to 15 is named by some query.
All inputs are finite; a program needn't handle non-finite values.
Results may differ from a plain program's by a relative error of at most 0.0018.
Values may be sent and summed in bfloat16 or wider, within the bound.
A program may use at most 128 MiB of HBM per device.

v0:
```python
import jax
import jax.numpy as jnp
from jax import lax
from jax.sharding import PartitionSpec as P

TASKS = 16


def score_rows(piece, store):
    return jnp.einsum(
        "lqk,lek->qe",
        piece.astype(jnp.float32),
        store,
        precision=lax.Precision.HIGHEST,
        preferred_element_type=jnp.float32,
    )


def masked_peak(scores, member):
    return jnp.max(jnp.where(member[:, :, None], scores[None, :, :], -jnp.inf), axis=1)


def on_device(store, queries, second_moment, layer_rate, query_task):
    factor = layer_rate[:, None, None] * lax.rsqrt(second_moment)[:, None, :]
    precond = (queries * factor).astype(jnp.bfloat16)
    gathered = lax.all_gather(precond, "dp", axis=1, tiled=True)
    partial_value = score_rows(gathered, store)
    task_ids = jnp.arange(TASKS, dtype=jnp.int32)
    member = query_task[:, 0][None, :] == task_ids[:, None]
    totals = lax.psum(partial_value, "layer")
    best = masked_peak(totals, member)
    return best


def solution(mesh):
    in_specs = (
        P("layer", ("groups", "dp"), None),
        P("layer", "dp", None),
        P("layer", None),
        P("layer"),
        P(),
    )
    out_specs = P(None, ("groups", "dp"))
    return jax.shard_map(
        on_device, mesh=mesh, in_specs=in_specs, out_specs=out_specs, check_vma=False
    )
```

profile of v0, /device:TPU:1, one launch (start us, length us, event | category | flops | bytes accessed | tf_op | source)
XLA Modules:
  0.0 97.7 jit_solution(2638390094635168920)
XLA Ops:
  6.5 0.0 copy-start
  6.5 0.0 all-gather.2.cloned.1.call-start
  7.2 0.7 rsqrt_multiply_fusion
  7.9 1.8 %multiply_convert_fusion = bf16[1,32,4096]{2,1,0:T(8,128)(2,1)} fusion(f32[1,32,4096]{2,1,0:T(8,128)} %param.6, f32[4096]{0:T(1024)S(1)} %bitcast.10), kind=kLoop, calls=%fused_computation.4 | loop fusion | flops 262144 | bytes 802816 | tf_op jit(solution)/shard_map/convert_element_type | solution.py:25
  9.8 0.0 all-gather.2.cloned.1.call-update
  9.8 0.0 all-reduce.2.cloned.1.call-start
  9.8 50.4 %all-gather.2.cloned.1.call-done = bf16[1,256,4096]{2,1,0:T(8,128)(2,1)} async-done(((bf16[1,32,4096]{2,1,0:T(8,128)(2,1)}), bf16[1,256,4096]{2,1,0:T(8,128)(2,1)}) %all-gather.2.cloned.1.call-update) | async-done | bytes 2097168 | tf_op jit(solution)/shard_map/all_gather | solution.py:26
  60.2 8.8 %fusion = f32[256,512]{1,0:T(8,128)} fusion(f32[1,512,4096]{2,1,0:T(8,128)} %param.5, bf16[1,256,4096]{2,1,0:T(8,128)(2,1)} %all-gather.2.cloned.1.call-done), kind=kOutput, calls=%fused_computation | convolution fusion | flops 6442450944 | bytes 11010048 | tf_op jit(solution)/shard_map/lqk,lek->qe/dot_general | solution.py:10
  69.1 0.0 all-reduce.2.cloned.1.call-update
  69.1 0.0 copy-done
  69.1 18.8 %all-reduce.2.cloned.1.call-done = f32[256,512]{1,0:T(8,128)} async-done(((f32[256,512]{1,0:T(8,128)}), f32[256,512]{1,0:T(8,128)}) %all-reduce.2.cloned.1.call-update) | async-done | bytes 524304 | tf_op jit(solution)/shard_map/psum | solution.py:30
  87.9 2.9 %select_reduce_fusion = f32[16,512]{1,0:T(8,128)} fusion(f32[256,512]{1,0:T(8,128)} %all-reduce.2.cloned.1.call-done, pred[16,256]{1,0:T(8,128)(4,1)S(1)} %iota_compare_fusion), kind=kLoop, calls=%fused_computation.2 | loop fusion | flops 4186112 | bytes 561152 | tf_op jit(solution)/shard_map/reduce_max | solution.py:20
  (1 shorter events, 0.0 us)
Async XLA Ops:
  6.5 62.5 %copy-start = (s32[256,1]{0,1:T(1,128)S(1)}, s32[256,1]{0,1:T(1,128)}, u32[]{:S(2)}) copy-start(s32[256,1]{0,1:T(1,128)} %param.9) | copy-start | bytes 3076
  6.5 53.7 %all-gather.2.cloned.1.call-start = ((), (), s32[]{:S(2)}) async-start(), calls=%async_computation | async-start | bytes 2359296 | tf_op jit(solution)/shard_map/all_gather | solution.py:26
  9.8 78.2 %all-reduce.2.cloned.1.call-start = ((), (), s32[]{:S(2)}) async-start(), calls=%async_computation.1 | async-start | bytes 1048576 | tf_op jit(solution)/shard_map/psum | solution.py:30
Sparse Core Ops, SparseCore 0:
  9.9 50.2 all-gather.1
  69.2 18.6 all-reduce.1
where the time goes:
time: 98.2 us; the launch traced here: 97.7 us
  waiting for transfers between devices  69.2 us (70%)
  between operations  14.1 us (14%)
  matrix products  8.85 us (9%)
  other arithmetic  5.5 us (6%)
    all_gather x1, waiting for transfers between devices, on_device(): gathered = lax.all_gather(precond, 'dp', axis=1, tiled=True)  50.4 us
    psum x1, waiting for transfers between devices, on_device(): totals = lax.psum(partial_value, 'layer')  18.8 us
    dot_general x1, matrix products, score_rows(): jnp.einsum('lqk,lek->qe', piece.astype(jnp.float32), store, precision=lax...  8.85 us
    reduce_max x1, other arithmetic, masked_peak(): jnp.max(jnp.where(member[:, :, None], scores[None, :, :], -jnp.inf), axis=1)  2.94 us
  transfers between devices with their start and end apart: 2, of which 2 were waited for; matrix products, arithmetic and copies ran while one was open for 0% of the time, Pallas kernels for 0%

commit v1 on v0

v1 whole, which is shorter than its diff:
```python
import functools

import jax
import jax.numpy as jnp
from jax import lax
from jax.experimental import pallas as pl
from jax.experimental.pallas import tpu as pltpu
from jax.sharding import PartitionSpec as P

TASKS = 16
QUARTERS = 4
MESH = pl.DeviceIdType.MESH


def kernel(
    length,
    store_ref,
    query_ref,
    moment_ref,
    rate_ref,
    task_ref,
    out_ref,
    raw,
    high,
    low,
    own,
    rows,
    acc,
    other,
    best,
    store_sem,
    query_sem,
    recv_sem,
    line_sem,
    plane_sem,
    pair_send,
    pair_recv,
):
    x = lax.axis_index("groups")
    dp = lax.axis_index("dp")
    core = lax.axis_index("layer")
    z, y = dp // 2, dp % 2
    parity = (x + y) % 2
    mine, theirs = 2 * parity, 2 * (1 - parity)
    width = raw.shape[2]
    to_x = {"groups": 1 - x}
    to_y = {"dp": z * 2 + 1 - y}
    to_core = {"layer": 1 - core}
    to_line = ({"dp": dp - 2}, {"dp": dp + 2})
    has_line = (z > 0, z < length - 1)

    get_query = pltpu.make_async_copy(query_ref.at[0], own, query_sem)
    get_query.start()
    get_store = [
        pltpu.make_async_copy(
            store_ref.at[0, :, pl.ds(i * width, width)], raw.at[i], store_sem.at[i]
        )
        for i in range(QUARTERS)
    ]
    for copy in get_store:
        copy.start()

    barrier = pltpu.get_barrier_semaphore()
    for peer in (to_x, to_y, to_core):
        pl.semaphore_signal(barrier, inc=1, device_id=peer, device_id_type=MESH)
    for way in range(2):

        @pl.when(has_line[way])
        def _():
            pl.semaphore_signal(
                barrier, inc=1, device_id=to_line[way], device_id_type=MESH
            )

    def chunk_copy(shard, quarter, send_sem, peer):
        return pltpu.make_async_remote_copy(
            src_ref=rows.at[shard, quarter],
            dst_ref=rows.at[shard, quarter],
            send_sem=send_sem,
            recv_sem=recv_sem.at[shard, quarter],
            device_id=peer,
            device_id_type=MESH,
        )

    def line(shard, quarter, way):
        return chunk_copy(shard, quarter, line_sem.at[shard, quarter, way], to_line[way])

    def plane(shard, quarter, peer):
        return chunk_copy(shard, quarter, plane_sem.at[shard, quarter], peer)

    def arrived(shard, quarter):
        plane(shard, quarter, to_x).wait_recv()

    def pair(block):
        return pltpu.make_async_remote_copy(
            src_ref=acc.at[block],
            dst_ref=other.at[block],
            send_sem=pair_send.at[block],
            recv_sem=pair_recv.at[block],
            device_id=to_core,
            device_id_type=MESH,
        )

    def piece(block, quarter):
        count = rows.shape[2]
        left = jnp.concatenate(
            [rows[2 * block, quarter], rows[2 * block + 1, quarter]], axis=0
        )
        dims = (((1,), (1,)), ((), ()))
        acc[block] += lax.dot_general(
            left, high[quarter], dims, preferred_element_type=jnp.float32
        ) + lax.dot_general(
            left, low[quarter], dims, preferred_element_type=jnp.float32
        )

    def convert(i):
        get_store[i].wait()
        step = 64

        def body(r, _):
            at = pl.ds(pl.multiple_of(r * step, step), step)
            value = raw[i, at, :]
            top = value.astype(jnp.bfloat16)
            high[i, at, :] = top
            low[i, at, :] = (value - top.astype(jnp.float32)).astype(jnp.bfloat16)
            return 0

        lax.fori_loop(0, raw.shape[1] // step, body, 0)

    def peak(block):
        pair(block).wait_recv()
        count = acc.shape[1]
        scores = acc[block] + other[block]
        tasks = task_ref[pl.ds(pl.multiple_of(block * count, count), count), :]
        tasks = jnp.broadcast_to(tasks, scores.shape)
        for t in range(TASKS):
            value = jnp.where(tasks == t, scores, -jnp.inf)
            value = jnp.max(value.reshape(count // 8, 8, scores.shape[1]), axis=0)
            best[t] = jnp.maximum(best[t], value)

    def finish(block, quarter):
        piece(block, quarter)
        pair(block).start()

    get_query.wait()
    me, mate = dp, z * 2 + 1 - y
    for i in range(QUARTERS):
        at = pl.ds(i * width, width)
        factor = rate_ref[0] * lax.rsqrt(moment_ref[:, at])
        rows[me, i] = (own[:, at] * factor).astype(jnp.bfloat16)

    waits = 3 + jnp.where(z > 0, 1, 0) + jnp.where(z < length - 1, 1, 0)
    pl.semaphore_wait(barrier, waits)

    for j in range(2):
        plane(me, theirs + j, to_y).start()
        for way in range(2):

            @pl.when(has_line[way])
            def _():
                line(me, mine + j, way).start()

    acc[...] = jnp.zeros_like(acc)
    best[...] = jnp.full_like(best, -jnp.inf)
    for j in range(2):
        convert(j)
        arrived(mate, mine + j)
        for way in range(2):

            @pl.when(has_line[way])
            def _():
                line(mate, mine + j, way).start()

        plane(mate, mine + j, to_x).start()
    convert(2)
    convert(3)
    piece(z, mine)
    piece(z, mine + 1)
    arrived(mate, theirs)
    piece(z, theirs)
    arrived(mate, theirs + 1)
    finish(z, theirs + 1)

    def source(far, way):
        return z - far if way == 0 else z + far

    def valid(src):
        return (src >= 0) & (src < length)

    def over_ways(far, action):
        def body(way, _):
            src = z + (2 * way - 1) * far

            @pl.when(valid(src))
            def _():
                action(src)

            return 0

        lax.fori_loop(0, 2, body, 0)

    def last_piece(src):
        arrived(2 * src, theirs + 1)
        arrived(2 * src + 1, theirs + 1)
        finish(src, theirs + 1)

    def round_of(far, _):
        for j in range(2):
            for side in range(2):
                for way in range(2):
                    src = source(far, way)
                    shard = 2 * src + side

                    @pl.when(valid(src))
                    def _():
                        arrived(shard, mine + j)

                        @pl.when(has_line[1 - way])
                        def _():
                            line(shard, mine + j, 1 - way).start()

                        plane(shard, mine + j, to_x if j == 0 else to_y).start()

            over_ways(far, lambda src: piece(src, mine + j))
            if j == 0:

                @pl.when(far > 1)
                def _():
                    over_ways(far - 1, last_piece)
            else:

                def early_piece(src):
                    arrived(2 * src, theirs)
                    arrived(2 * src + 1, theirs)
                    piece(src, theirs)

                over_ways(far, early_piece)

                @pl.when(far == 1)
                def _():
                    peak(z)

                @pl.when(far > 1)
                def _():
                    over_ways(far - 1, peak)

        return 0

    lax.fori_loop(1, length, round_of, 0)
    over_ways(length - 1, last_piece)
    over_ways(length - 1, peak)

    for t in range(TASKS):
        out_ref[pl.ds(t, 1), :] = jnp.max(best[t], axis=0, keepdims=True)

    for j in range(2):
        plane(me, theirs + j, to_y).wait_send()
        plane(mate, mine + j, to_x).wait_send()
        for way in range(2):

            @pl.when(has_line[way])
            def _():
                line(me, mine + j, way).wait_send()
                line(mate, mine + j, way).wait_send()

    pair(z).wait_send()

    def drain(far, _):
        for way in range(2):
            src = source(far, way)

            @pl.when(valid(src))
            def _():
                pair(src).wait_send()
                for j in range(2):
                    for side in range(2):
                        shard = 2 * src + side
                        plane(shard, mine + j, to_x if j == 0 else to_y).wait_send()

                        @pl.when(has_line[1 - way])
                        def _():
                            line(shard, mine + j, 1 - way).wait_send()

        return 0

    lax.fori_loop(1, length, drain, 0)


def on_device(mesh_dp, store, queries, second_moment, layer_rate, query_task):
    length = mesh_dp // 2
    examples, depth = store.shape[1], store.shape[2]
    each = queries.shape[1]
    width = depth // QUARTERS
    dma, vmem = pltpu.SemaphoreType.DMA, pltpu.VMEM
    return pl.pallas_call(
        functools.partial(kernel, length),
        out_shape=jax.ShapeDtypeStruct((TASKS, examples), jnp.float32),
        in_specs=[
            pl.BlockSpec(memory_space=pl.ANY),
            pl.BlockSpec(memory_space=pl.ANY),
            pl.BlockSpec(memory_space=pltpu.VMEM),
            pl.BlockSpec(memory_space=pltpu.SMEM),
            pl.BlockSpec(memory_space=pltpu.VMEM),
        ],
        out_specs=pl.BlockSpec(memory_space=pltpu.VMEM),
        scratch_shapes=[
            vmem((QUARTERS, examples, width), jnp.float32),
            vmem((QUARTERS, examples, width), jnp.bfloat16),
            vmem((QUARTERS, examples, width), jnp.bfloat16),
            vmem((each, depth), jnp.float32),
            vmem((mesh_dp, QUARTERS, each, width), jnp.bfloat16),
            vmem((length, 2 * each, examples), jnp.float32),
            vmem((length, 2 * each, examples), jnp.float32),
            vmem((TASKS, 8, examples), jnp.float32),
            dma((QUARTERS,)),
            dma,
            dma((mesh_dp, QUARTERS)),
            dma((mesh_dp, QUARTERS, 2)),
            dma((mesh_dp, QUARTERS)),
            dma((length,)),
            dma((length,)),
        ],
        compiler_params=pltpu.CompilerParams(
            collective_id=0, has_side_effects=True, vmem_limit_bytes=56 * 1024 * 1024
        ),
        cost_estimate=pl.CostEstimate(
            flops=4 * each * mesh_dp * examples * depth,
            bytes_accessed=4 * (examples + each) * depth,
            transcendentals=depth,
        ),
    )(store, queries, second_moment, layer_rate, query_task)


def solution(mesh):
    in_specs = (
        P("layer", ("groups", "dp"), None),
        P("layer", "dp", None),
        P("layer", None),
        P("layer"),
        P(),
    )
    out_specs = P(None, ("groups", "dp"))
    return jax.shard_map(
        functools.partial(on_device, mesh.shape["dp"]),
        mesh=mesh,
        in_specs=in_specs,
        out_specs=out_specs,
        check_vma=False,
    )
```

time: 98.2 us -> 40.6 us (0.41)
  waiting for transfers between devices: 69.2 us -> 0 us
  Pallas kernels: 0 us -> 36.8 us
  between operations: 14.1 us -> 0.66 us
  matrix products: 8.85 us -> 0 us
  other arithmetic: 5.5 us -> 0 us
  local copies, waits for them, and re-layouts: 0.01 us -> 2.83 us
    all_gather x1 -> x0, waiting for transfers between devices: 50.4 us -> none  [on_device(): gathered = lax.all_gather(precond, 'dp', axis=1, tiled=True)]
    pallas_call x0 -> x1, Pallas kernels: none -> 36.8 us  [on_device(): pl.pallas_call(functools.partial(kernel, length), out_shape=jax.ShapeDtyp...]
    psum x1 -> x0, waiting for transfers between devices: 18.8 us -> none  [on_device(): totals = lax.psum(partial_value, 'layer')]
    dot_general x1 -> x0, matrix products: 8.85 us -> none  [score_rows(): jnp.einsum('lqk,lek->qe', piece.astype(jnp.float32), store, precision=lax...]
    reduce_max x1 -> x0, other arithmetic: 2.94 us -> none  [masked_peak(): jnp.max(jnp.where(member[:, :, None], scores[None, :, :], -jnp.inf), axis=1)]
    unnamed x2, local copies, waits for them, and re-layouts: 0.01 us -> 2.83 us
    convert_element_type x1 -> x0, other arithmetic: 1.81 us -> none  [on_device(): precond = (queries * factor).astype(jnp.bfloat16)]
  transfers between devices with their start and end apart: 2 -> 0, of which waited for: 2 -> 0; matrix products, arithmetic and copies ran while one was open for 0% -> 0% of each run, Pallas kernels for 0% -> 0%
where the time goes in v1:
time: 40.6 us; the launch traced here: 40.3 us
  Pallas kernels  36.8 us (91%)
  local copies, waits for them, and re-layouts  2.83 us (7%)
  between operations  0.66 us (2%)
    pallas_call x1, Pallas kernels, on_device(): pl.pallas_call(functools.partial(kernel, length), out_shape=jax.ShapeDtyp...  36.8 us
    unnamed x2, local copies, waits for them, and re-layouts  2.83 us

profile of v1, /device:TPU:1, one launch (start us, length us, event | category | flops | bytes accessed | tf_op | source)
XLA Modules:
  0.0 40.3 jit_solution(12697576346228539551)
XLA Ops:
  0.7 1.5 %copy.6.task_ref = s32[256,1]{1,0:T(8,128)} copy(s32[256,1]{0,1:T(1,128)} %param.9) | data formatting | bytes 2048 | tf_op args[4]
  2.1 36.8 %shard_map.55 = f32[16,512]{1,0:T(8,128)} custom-call(f32[1,512,4096]{2,1,0:T(8,128)} %store_ref.1, f32[1,32,4096]{2,1,0:T(8,128)} %query_ref.1, f32[1,4096]{1,0:T(1,128)} %moment_ref.1, f32[1]{0:T(128)S(6)} %copy.8.rate_ref, s32[256,1]{1,0:T(8,128)} %copy.6.task_ref), custom_call_target="tpu_custom_call" | custom-call | flops 2147483648 | bytes 8912896 | tf_op jit(solution)/shard_map/pallas_call | solution.py:294
  39.0 1.4 %copy.9 = f32[16,512]{1,0:T(8,128)} copy(f32[16,512]{1,0:T(8,128)} %shard_map.55) | data formatting | bytes 65536

commit v2 on v1

v2 whole, which is shorter than its diff:
```python
import functools

import jax
import jax.numpy as jnp
from jax import lax
from jax.experimental import pallas as pl
from jax.experimental.pallas import tpu as pltpu
from jax.sharding import PartitionSpec as P

TASKS = 16
QUARTERS = 4
PARTS = 1
LANES = 128
MESH = pl.DeviceIdType.MESH


def kernel(
    length,
    store_ref,
    query_ref,
    moment_ref,
    rate_ref,
    task_ref,
    out_ref,
    raw,
    high,
    low,
    own,
    rows,
    acc,
    other,
    best,
    columns,
    store_sem,
    query_sem,
    recv_sem,
    line_sem,
    plane_sem,
    pair_send,
    pair_recv,
):
    x = lax.axis_index("groups")
    dp = lax.axis_index("dp")
    core = lax.axis_index("layer")
    z, y = dp // 2, dp % 2
    parity = (x + y) % 2
    mine, theirs = 2 * parity, 2 * (1 - parity)
    width = raw.shape[2]
    edge = (z == 0) | (z == length - 1)
    quad, quad_x = mine + x, theirs + 1 - x
    quad_y, quad_far = theirs + x, mine + 1 - x
    to_x = {"groups": 1 - x}
    to_y = {"dp": z * 2 + 1 - y}
    to_core = {"layer": 1 - core}
    to_line = ({"dp": dp - 2}, {"dp": dp + 2})
    has_line = (z > 0, z < length - 1)
    to_edge = (z == 1, z == length - 2)
    starts_line = [
        [has_line[way] & ((j == x) | ~to_edge[way]) for way in range(2)]
        for j in range(2)
    ]

    get_query = pltpu.make_async_copy(query_ref.at[0], own, query_sem)
    get_query.start()

    def get_store(i):
        at = pl.ds(pl.multiple_of(i * width, width), width)
        return pltpu.make_async_copy(store_ref.at[0, :, at], raw.at[i], store_sem.at[i])

    barrier = pltpu.get_barrier_semaphore()
    for peer in (to_x, to_y, to_core):
        pl.semaphore_signal(barrier, inc=1, device_id=peer, device_id_type=MESH)
    for way in range(2):

        @pl.when(has_line[way])
        def _():
            pl.semaphore_signal(
                barrier, inc=1, device_id=to_line[way], device_id_type=MESH
            )

    part_rows = rows.shape[2] // PARTS

    def chunk_copy(shard, quarter, part, send_sem, peer):
        place = rows.at[shard, quarter, pl.ds(part * part_rows, part_rows)]
        return pltpu.make_async_remote_copy(
            src_ref=place,
            dst_ref=place,
            send_sem=send_sem,
            recv_sem=recv_sem.at[shard, quarter, part],
            device_id=peer,
            device_id_type=MESH,
        )

    def line(shard, quarter, part, way):
        send_sem = line_sem.at[shard, quarter, part, way]
        return chunk_copy(shard, quarter, part, send_sem, to_line[way])

    def plane(shard, quarter, part, axis):
        send_sem = plane_sem.at[shard, quarter, part, axis]
        return chunk_copy(shard, quarter, part, send_sem, to_y if axis else to_x)

    def arrived_part(shard, quarter, part):
        plane(shard, quarter, part, 0).wait_recv()

    def arrived(shard, quarter):
        for part in range(PARTS):
            arrived_part(shard, quarter, part)

    def sent_plane(shard, quarter, axis):
        for part in range(PARTS):
            plane(shard, quarter, part, axis).wait_send()

    def sent_line(shard, quarter, way):
        for part in range(PARTS):
            line(shard, quarter, part, way).wait_send()

    def pair(block):
        return pltpu.make_async_remote_copy(
            src_ref=acc.at[block],
            dst_ref=other.at[block],
            send_sem=pair_send.at[block],
            recv_sem=pair_recv.at[block],
            device_id=to_core,
            device_id_type=MESH,
        )

    def piece(block, quarter):
        left = jnp.concatenate(
            [rows[2 * block, quarter], rows[2 * block + 1, quarter]], axis=0
        )
        dims = (((1,), (0,)), ((), ()))
        acc[block] += lax.dot_general(
            left, high[quarter], dims, preferred_element_type=jnp.float32
        ) + lax.dot_general(
            left, low[quarter], dims, preferred_element_type=jnp.float32
        )

    def convert(i):
        get_store(i).wait()
        def body(r, _):
            at = pl.ds(pl.multiple_of(r * LANES, LANES), LANES)
            value = raw[i, at, :].T
            top = value.astype(jnp.bfloat16)
            high[i, :, at] = top
            low[i, :, at] = (value - top.astype(jnp.float32)).astype(jnp.bfloat16)
            return 0

        lax.fori_loop(0, raw.shape[1] // LANES, body, 0)

    def peak(block):
        pair(block).wait_recv()
        count = acc.shape[1]
        scores = acc[block] + other[block]
        tasks = columns[pl.ds(pl.multiple_of(block * count, count), count), :]
        tasks = jnp.concatenate([tasks] * (scores.shape[1] // LANES), axis=1)
        for t in range(TASKS):
            value = jnp.where(tasks == t, scores, -jnp.inf)
            value = jnp.max(value.reshape(count // 8, 8, scores.shape[1]), axis=0)
            best[t] = jnp.maximum(best[t], value)

    def finish(block, quarter):
        piece(block, quarter)
        pair(block).start()

    get_query.wait()
    me, mate = dp, z * 2 + 1 - y
    for i in range(QUARTERS):
        at = pl.ds(i * width, width)
        factor = rate_ref[0] * lax.rsqrt(moment_ref[:, at])
        rows[me, i] = (own[:, at] * factor).astype(jnp.bfloat16)

    waits = 3 + jnp.where(z > 0, 1, 0) + jnp.where(z < length - 1, 1, 0)
    pl.semaphore_wait(barrier, waits)

    for i in range(QUARTERS):
        get_store(i).start()

    for j in range(2):
        for part in range(PARTS):
            plane(me, theirs + j, part, 1).start()
            for way in range(2):

                @pl.when(starts_line[j][way])
                def _():
                    line(me, mine + j, part, way).start()

    for i in range(columns.shape[0] // LANES):
        at = pl.ds(i * LANES, LANES)
        columns[at, :] = jnp.broadcast_to(task_ref[:, at], (LANES, LANES)).T
    acc[...] = jnp.zeros_like(acc)
    best[...] = jnp.full_like(best, -jnp.inf)
    for j in range(2):
        for part in range(PARTS):
            arrived_part(mate, mine + j, part)
            for way in range(2):

                @pl.when(starts_line[j][way])
                def _():
                    line(mate, mine + j, part, way).start()

            plane(mate, mine + j, part, 0).start()

    def convert_all():
        def body(i, _):
            convert(i)
            return 0

        lax.fori_loop(0, QUARTERS, body, 0)

    def own_plane():
        def body(i, _):
            quarter = jnp.where(i < 2, mine + i, theirs + i - 2)

            @pl.when(i >= 2)
            def _():
                arrived(mate, quarter)

            piece(z, quarter)
            return 0

        lax.fori_loop(0, QUARTERS, body, 0)
        pair(z).start()

    def source(far, way):
        return z - far if way == 0 else z + far

    def valid(src):
        return (src >= 0) & (src < length)

    def over_ways(far, action):
        def body(way, _):
            src = z + (2 * way - 1) * far

            @pl.when(valid(src))
            def _():
                action(src)

            return 0

        lax.fori_loop(0, 2, body, 0)

    def last_piece(far):
        quarter = jnp.where(edge & (far == 1), quad_far, theirs + 1)

        def body(src):
            arrived(2 * src, quarter)
            arrived(2 * src + 1, quarter)
            finish(src, quarter)

        return body

    def edge_round():
        src = jnp.where(z == 0, 1, length - 2)
        first, second = 2 * src + y, 2 * src + 1 - y

        def spread(shard):
            for part in range(PARTS):
                arrived_part(shard, quad, part)
                plane(shard, quad, part, 0).start()
                plane(shard, quad, part, 1).start()

        spread(first)
        convert_all()
        spread(second)
        own_plane()
        for part in range(PARTS):
            arrived_part(2 * src, quad_y, part)
            plane(2 * src, quad_y, part, 0).start()
            arrived_part(2 * src + 1, quad_x, part)
            plane(2 * src + 1, quad_x, part, 1).start()
        arrived(2 * src + 1, quad_y)
        arrived(2 * src, quad_x)

        def body(i, _):
            quarter = jnp.where(i == 0, quad, jnp.where(i == 1, quad_y, quad_x))
            piece(src, quarter)
            return 0

        lax.fori_loop(0, 3, body, 0)

    def pass_on(far, side, j):
        for part in range(PARTS):
            for way in range(2):
                src = source(far, way)
                shard = 2 * src + side

                @pl.when(valid(src))
                def _():
                    arrived_part(shard, mine + j, part)

                    @pl.when(has_line[1 - way])
                    def _():
                        line(shard, mine + j, part, 1 - way).start()

                    plane(shard, mine + j, part, j).start()

    def plain_round(far):
        pass_on(far, y, 0)
        pass_on(far, y, 1)

        @pl.when(far == 1)
        def _():
            convert_all()

        @pl.when(far > 1)
        def _():
            over_ways(far - 1, last_piece(far - 1))

        pass_on(far, 1 - y, 0)
        pass_on(far, 1 - y, 1)

        @pl.when(far == 1)
        def _():
            own_plane()

        def pieces(src):
            def body(i, _):
                quarter = jnp.where(i < 2, mine + i, theirs)

                @pl.when(i == 2)
                def _():
                    arrived(2 * src, theirs)
                    arrived(2 * src + 1, theirs)

                piece(src, quarter)
                return 0

            lax.fori_loop(0, 3, body, 0)

        over_ways(far, pieces)

    def round_of(far, _):
        near_edge = edge & (far == 1)
        pl.when(near_edge)(edge_round)
        pl.when(~near_edge)(lambda: plain_round(far))

        @pl.when(far == 1)
        def _():
            peak(z)

        @pl.when(far > 1)
        def _():
            over_ways(far - 1, peak)

        return 0

    lax.fori_loop(1, length, round_of, 0)
    over_ways(length - 1, last_piece(length - 1))
    over_ways(length - 1, peak)

    for t in range(TASKS):
        out_ref[pl.ds(t, 1), :] = jnp.max(best[t], axis=0, keepdims=True)

    for j in range(2):
        sent_plane(me, theirs + j, 1)
        sent_plane(mate, mine + j, 0)
        for way in range(2):

            @pl.when(starts_line[j][way])
            def _():
                sent_line(me, mine + j, way)
                sent_line(mate, mine + j, way)

    pair(z).wait_send()

    def drain(far, _):
        for way in range(2):
            src = source(far, way)

            @pl.when(valid(src))
            def _():
                pair(src).wait_send()
                near_edge = edge & (far == 1)

                @pl.when(near_edge)
                def _():
                    for side in range(2):
                        sent_plane(2 * src + side, quad, 0)
                        sent_plane(2 * src + side, quad, 1)
                    sent_plane(2 * src, quad_y, 0)
                    sent_plane(2 * src + 1, quad_x, 1)

                @pl.when(~near_edge)
                def _():
                    for j in range(2):
                        for side in range(2):
                            shard = 2 * src + side
                            sent_plane(shard, mine + j, j)

                            @pl.when(has_line[1 - way])
                            def _():
                                sent_line(shard, mine + j, 1 - way)

        return 0

    lax.fori_loop(1, length, drain, 0)


def on_device(mesh_dp, store, queries, second_moment, layer_rate, query_task):
    length = mesh_dp // 2
    examples, depth = store.shape[1], store.shape[2]
    each = queries.shape[1]
    width = depth // QUARTERS
    dma, vmem = pltpu.SemaphoreType.DMA, pltpu.VMEM
    return pl.pallas_call(
        functools.partial(kernel, length),
        out_shape=jax.ShapeDtypeStruct((TASKS, examples), jnp.float32),
        in_specs=[
            pl.BlockSpec(memory_space=pl.ANY),
            pl.BlockSpec(memory_space=pl.ANY),
            pl.BlockSpec(memory_space=pltpu.VMEM),
            pl.BlockSpec(memory_space=pltpu.SMEM),
            pl.BlockSpec(memory_space=pltpu.VMEM),
        ],
        out_specs=pl.BlockSpec(memory_space=pltpu.VMEM),
        scratch_shapes=[
            vmem((QUARTERS, examples, width), jnp.float32),
            vmem((QUARTERS, width, examples), jnp.bfloat16),
            vmem((QUARTERS, width, examples), jnp.bfloat16),
            vmem((each, depth), jnp.float32),
            vmem((mesh_dp, QUARTERS, each, width), jnp.bfloat16),
            vmem((length, 2 * each, examples), jnp.float32),
            vmem((length, 2 * each, examples), jnp.float32),
            vmem((TASKS, 8, examples), jnp.float32),
            vmem((each * mesh_dp, LANES), jnp.int32),
            dma((QUARTERS,)),
            dma,
            dma((mesh_dp, QUARTERS, PARTS)),
            dma((mesh_dp, QUARTERS, PARTS, 2)),
            dma((mesh_dp, QUARTERS, PARTS, 2)),
            dma((length,)),
            dma((length,)),
        ],
        compiler_params=pltpu.CompilerParams(
            collective_id=0, has_side_effects=True, vmem_limit_bytes=56 * 1024 * 1024
        ),
        cost_estimate=pl.CostEstimate(
            flops=4 * each * mesh_dp * examples * depth,
            bytes_accessed=4 * (examples + each) * depth,
            transcendentals=depth,
        ),
    )(store, queries, second_moment, layer_rate, query_task.reshape(1, -1))


def solution(mesh):
    in_specs = (
        P("layer", ("groups", "dp"), None),
        P("layer", "dp", None),
        P("layer", None),
        P("layer"),
        P(),
    )
    out_specs = P(None, ("groups", "dp"))
    return jax.shard_map(
        functools.partial(on_device, mesh.shape["dp"]),
        mesh=mesh,
        in_specs=in_specs,
        out_specs=out_specs,
        check_vma=False,
    )
```

time: 40.6 us -> 35.5 us (0.87)
  Pallas kernels: 36.8 us -> 33.2 us
  local copies, waits for them, and re-layouts: 2.83 us -> 1.38 us
    pallas_call x1, Pallas kernels: 36.8 us -> 33.2 us  [on_device(): pl.pallas_call(functools.partial(kernel, length), out_shape=jax.ShapeDtyp...]
    unnamed x2 -> x1, local copies, waits for them, and re-layouts: 2.83 us -> 1.38 us
where the time goes in v2:
time: 35.5 us; the launch traced here: 35.2 us
  Pallas kernels  33.2 us (94%)
  local copies, waits for them, and re-layouts  1.38 us (4%)
  between operations  0.66 us (2%)
    pallas_call x1, Pallas kernels, on_device(): pl.pallas_call(functools.partial(kernel, length), out_shape=jax.ShapeDtyp...  33.2 us
    unnamed x1, local copies, waits for them, and re-layouts  1.38 us

profile of v2, /device:TPU:1, one launch (start us, length us, event | category | flops | bytes accessed | tf_op | source)
XLA Modules:
  0.0 35.2 jit_solution(1229908146350089378)
XLA Ops:
  0.7 33.2 %shard_map.55 = f32[16,512]{1,0:T(8,128)} custom-call(f32[1,512,4096]{2,1,0:T(8,128)} %store_ref.1, f32[1,32,4096]{2,1,0:T(8,128)} %query_ref.1, f32[1,4096]{1,0:T(1,128)} %moment_ref.1, f32[1]{0:T(128)S(6)} %copy.7.rate_ref, s32[1,256]{1,0:T(1,128)} %bitcast.1), custom_call_target="tpu_custom_call" | custom-call | flops 2147483648 | bytes 8912896 | tf_op jit(solution)/shard_map/pallas_call | solution.py:405
  33.8 1.4 %copy.8 = f32[16,512]{1,0:T(8,128)} copy(f32[16,512]{1,0:T(8,128)} %shard_map.55) | data formatting | bytes 65536

commit v3 on v2

--- a/solution.py
+++ b/solution.py
@@ -302,12 +302,12 @@
         def _():
             convert_all()
 
-        @pl.when(far > 1)
-        def _():
-            over_ways(far - 1, last_piece(far - 1))
-
         pass_on(far, 1 - y, 0)
         pass_on(far, 1 - y, 1)
+
+        @pl.when(far > 1)
+        def _():
+            over_ways(far - 1, last_piece(far - 1))
 
         @pl.when(far == 1)
         def _():

time: 35.5 us -> 35 us (0.986)
  Pallas kernels: 33.2 us -> 32.7 us
    pallas_call x1, Pallas kernels: 33.2 us -> 32.7 us  [on_device(): pl.pallas_call(functools.partial(kernel, length), out_shape=jax.ShapeDtyp...]
where the time goes in v3:
time: 35 us; the launch traced here: 34.7 us
  Pallas kernels  32.7 us (93%)
  local copies, waits for them, and re-layouts  1.38 us (4%)
  between operations  0.66 us (2%)
    pallas_call x1, Pallas kernels, on_device(): pl.pallas_call(functools.partial(kernel, length), out_shape=jax.ShapeDtyp...  32.7 us
    unnamed x1, local copies, waits for them, and re-layouts  1.38 us

profile of v3, /device:TPU:1, one launch (start us, length us, event | category | flops | bytes accessed | tf_op | source)
XLA Modules:
  0.0 34.7 jit_solution(5394434043602547137)
XLA Ops:
  0.7 32.7 %shard_map.55 = f32[16,512]{1,0:T(8,128)} custom-call(f32[1,512,4096]{2,1,0:T(8,128)} %store_ref.1, f32[1,32,4096]{2,1,0:T(8,128)} %query_ref.1, f32[1,4096]{1,0:T(1,128)} %moment_ref.1, f32[1]{0:T(128)S(6)} %copy.7.rate_ref, s32[1,256]{1,0:T(1,128)} %bitcast.1), custom_call_target="tpu_custom_call" | custom-call | flops 2147483648 | bytes 8912896 | tf_op jit(solution)/shard_map/pallas_call | solution.py:405
  33.4 1.4 %copy.8 = f32[16,512]{1,0:T(8,128)} copy(f32[16,512]{1,0:T(8,128)} %shard_map.55) | data formatting | bytes 65536

commit v4 on v3

--- a/solution.py
+++ b/solution.py
@@ -302,10 +302,14 @@
         def _():
             convert_all()
 
+        @pl.when((far > 1) & (far == length - 1))
+        def _():
+            over_ways(far - 1, last_piece(far - 1))
+
         pass_on(far, 1 - y, 0)
         pass_on(far, 1 - y, 1)
 
-        @pl.when(far > 1)
+        @pl.when((far > 1) & (far < length - 1))
         def _():
             over_ways(far - 1, last_piece(far - 1))
 

time: 35 us -> 35 us (level)
  no operation moved by 1% of the time
where the time goes in v4:
time: 35 us; the launch traced here: 34.7 us
  Pallas kernels  32.7 us (93%)
  local copies, waits for them, and re-layouts  1.38 us (4%)
  between operations  0.66 us (2%)
    pallas_call x1, Pallas kernels, on_device(): pl.pallas_call(functools.partial(kernel, length), out_shape=jax.ShapeDtyp...  32.7 us
    unnamed x1, local copies, waits for them, and re-layouts  1.38 us

profile of v4, /device:TPU:1, one launch (start us, length us, event | category | flops | bytes accessed | tf_op | source)
XLA Modules:
  0.0 34.7 jit_solution(687385205117714685)
XLA Ops:
  0.7 32.7 %shard_map.55 = f32[16,512]{1,0:T(8,128)} custom-call(f32[1,512,4096]{2,1,0:T(8,128)} %store_ref.1, f32[1,32,4096]{2,1,0:T(8,128)} %query_ref.1, f32[1,4096]{1,0:T(1,128)} %moment_ref.1, f32[1]{0:T(128)S(6)} %copy.7.rate_ref, s32[1,256]{1,0:T(1,128)} %bitcast.1), custom_call_target="tpu_custom_call" | custom-call | flops 2147483648 | bytes 8912896 | tf_op jit(solution)/shard_map/pallas_call | solution.py:409
  33.4 1.4 %copy.8 = f32[16,512]{1,0:T(8,128)} copy(f32[16,512]{1,0:T(8,128)} %shard_map.55) | data formatting | bytes 65536
